TPU v7x, 512 devices: a whole 4x8x8 slice. The times are simulated.
512 devices in a mesh: seq: 128 (over y, z, core), head: 4 (over x).
Axes of the slice: x: 4, y: 8, z: 8, core: 2. Of those that a mesh axis runs over, the one named last changes fastest.
Arguments:
- routed_qkv: bfloat16 [3, 32768, 1024], P(None, 'seq', 'head'), may hold values from -64 to 64
- local_qkv: bfloat16 [3, 32768, 3072], P(None, 'seq', 'head'), may hold values from -64 to 64
- cluster_ids: int32 [8, 32768, 1], P('head', 'seq'), may hold values from 0 to 255; in each aligned block of 256 rows (0 to 255, 256 to 511, ..., all dimensions but the last counted through in order) at most 2 rows name the same one
- wo_routed: bfloat16 [1024, 4096], P('head', 'seq'), may hold values from -0.09375 to 0.09375
- wo_local: bfloat16 [3072, 4096], P('head', 'seq'), may hold values from -0.09375 to 0.09375
Outputs:
- layer_out: bfloat16 [32768, 4096], P('seq', 'head')
Inputs may be any that keep to these rules, and one draw needn't show every extreme that they name: `cluster_ids`: in each routed head, no cluster holds more than 2 of the 256 tokens of one index of seq (aligned blocks of 256 rows), and some cluster holds exactly 2 of them.
All inputs are finite; a program needn't handle non-finite values.
Results may differ from a plain program's by a relative error of at most 0.0095.
Values may be sent and summed in bfloat16 or wider, within the bound.
A program may use at most 64 MiB of HBM per device.

v0:
```python
import math
import jax
import jax.numpy as jnp
from jax import lax
from jax.sharding import PartitionSpec as P

HD = 128
WIN = 256
CL_DEV = 2
EMPTY = 128.0


def shifted(block, axis, distance):
    devices = range(lax.axis_size(axis))
    route = [(i - distance, i) for i in devices if i - distance in devices]
    return lax.ppermute(block, axis, route)


def attend(query, keys, values, allowed):
    scores = jnp.einsum("...qd,...kd->...qk", query, keys, preferred_element_type=jnp.float32) * (
        1.0 / math.sqrt(HD)
    )
    scores = jnp.where(allowed, scores, jnp.float32(-1e30))
    largest = jnp.max(scores, axis=-1, keepdims=True)
    raised = jnp.exp(scores - largest)
    weights = (raised / jnp.sum(raised, axis=-1, keepdims=True)).astype(jnp.bfloat16)
    return jnp.einsum(
        "...qk,...kd->...qd", weights, values, preferred_element_type=jnp.float32
    ).astype(jnp.bfloat16)


def on_device(routed_qkv, local_qkv, cluster_ids, wo_routed, wo_local):
    seq_count = lax.axis_size("seq")
    seq_place = lax.axis_index("seq")
    tok_rows = routed_qkv.shape[1]
    routed_count = cluster_ids.shape[0]
    local_count = local_qkv.shape[2] // HD
    cluster_total = CL_DEV * seq_count
    most_slots = max(2, 2 * tok_rows // cluster_total)
    proj_rows = jnp.concatenate([wo_routed, wo_local], axis=0)
    head_rows = (
        routed_qkv.reshape(3, tok_rows, routed_count, HD)
        .transpose(2, 1, 0, 3)
        .reshape(routed_count, tok_rows, 3 * HD)
    )
    cluster = cluster_ids[:, :, 0]
    order = jnp.arange(tok_rows, dtype=jnp.int32)
    same = (cluster[:, :, None] == cluster[:, None, :]) & (
        order[None, None, :] < order[None, :, None]
    )
    rank = jnp.sum(same.astype(jnp.int32), axis=2)
    slot_index = cluster * most_slots + rank
    slot_total = cluster_total * most_slots
    slot_names = jnp.arange(slot_total, dtype=jnp.int32)
    place = (slot_names[None, :, None] == slot_index[:, None, :]).astype(jnp.bfloat16)
    filled = jnp.sum(place.astype(jnp.float32), axis=2, keepdims=True)
    send_rows = (
        jnp.einsum("hst,htd->hsd", place, head_rows, preferred_element_type=jnp.float32)
        + (1.0 - filled) * EMPTY
    ).astype(jnp.bfloat16)
    rows = lax.all_to_all(send_rows, "seq", split_axis=1, concat_axis=1, tiled=True)
    count = rows.shape[0]
    slots = rows.shape[1]
    group = seq_count * most_slots
    members = (
        rows.reshape(count, seq_count, CL_DEV, most_slots, 3 * HD)
        .transpose(0, 2, 1, 3, 4)
        .reshape(count, CL_DEV, group, 3 * HD)
    )
    present = members[..., HD] < EMPTY / 2
    slot_order = jnp.arange(group, dtype=jnp.int32)
    allowed = present[..., None, :] & (slot_order[None, :] <= slot_order[:, None])
    result = attend(members[..., :HD], members[..., HD : 2 * HD], members[..., 2 * HD :], allowed)
    answered = (
        result.reshape(count, CL_DEV, seq_count, most_slots, HD)
        .transpose(0, 2, 1, 3, 4)
        .reshape(count, slots, HD)
    )
    returned = lax.all_to_all(answered, "seq", split_axis=1, concat_axis=1, tiled=True)
    picked = jnp.einsum("hst,hsd->htd", place, returned, preferred_element_type=jnp.float32).astype(
        jnp.bfloat16
    )
    routed_attn = picked.transpose(1, 0, 2).reshape(tok_rows, routed_count * HD)
    heads = local_qkv.reshape(3, tok_rows, local_count, HD).transpose(0, 2, 1, 3)
    tail = jnp.stack([heads[1], heads[2]])
    earlier = shifted(tail, "seq", 1)
    keys = jnp.concatenate([earlier[0], heads[1]], axis=1)
    values = jnp.concatenate([earlier[1], heads[2]], axis=1)
    key_pos = seq_place * tok_rows - WIN + jnp.arange(WIN + tok_rows, dtype=jnp.int32)
    query_pos = seq_place * tok_rows + jnp.arange(tok_rows, dtype=jnp.int32)
    allowed = (
        (key_pos[None, :] >= 0)
        & (key_pos[None, :] <= query_pos[:, None])
        & (key_pos[None, :] > query_pos[:, None] - WIN)
    )
    result = attend(heads[0], keys, values, allowed[None])
    local_attn = result.transpose(1, 0, 2).reshape(tok_rows, local_count * HD)
    joined = jnp.concatenate([routed_attn, local_attn], axis=1)
    terms = jnp.dot(
        joined,
        lax.all_gather(proj_rows, "seq", axis=1, tiled=True),
        preferred_element_type=jnp.float32,
    )
    rounded = terms.astype(jnp.bfloat16)
    return (
        lax.psum_scatter(rounded, "head", scatter_dimension=1, tiled=True)
        .astype(jnp.float32)
        .astype(jnp.bfloat16)
    )


def solution(mesh):
    placed = (
        P(None, "seq", "head"),
        P(None, "seq", "head"),
        P("head", "seq", None),
        P("head", "seq"),
        P("head", "seq"),
    )
    return jax.shard_map(
        on_device, mesh=mesh, in_specs=placed, out_specs=P("seq", "head"), check_vma=False
    )
```

profile of v0, /device:TPU:1, one launch (start us, length us, event | category | flops | bytes accessed | tf_op | source)
XLA Modules:
  0.0 167.3 jit_solution(8494341244411517680)
XLA Ops:
  6.5 1.4 pad_maximum_fusion
  8.0 0.7 copy.70
  8.7 1.3 copy.45
  10.0 0.2 convert_reduce_fusion.1
  10.3 0.7 multiply_add_fusion
  10.9 0.2 convert_reduce_fusion
  11.2 0.4 add_convert_fusion
  11.6 1.7 %copy.48 = bf16[2,512,384]{2,0,1:T(2,128)(2,1)} copy(bf16[2,512,384]{2,1,0:T(8,128)(2,1)S(1)} %add_convert_fusion) | data formatting | bytes 1572864 | tf_op jit(solution)/shard_map/convert_element_type | solution.py:60
  13.3 18.4 %all-to-all-start = ((bf16[2,512,384]{2,0,1:T(2,128)(2,1)}), bf16[2,512,384]{2,0,1:T(2,128)(2,1)S(1)}, u32[]{:S(2)}, u32[]{:S(2)}) async-start(bf16[2,512,384]{2,0,1:T(2,128)(2,1)} %copy.48), calls=%async_computation | async-start | bytes 1572864 | tf_op jit(solution)/shard_map/all_to_all | solution.py:61
  31.8 0.6 copy.54
  32.4 0.7 copy.55
  33.2 3.5 %collective-permute-start = (bf16[2,6,256,128]{3,2,1,0:T(8,128)(2,1)S(1)}, bf16[2,6,256,128]{3,2,1,0:T(8,128)(2,1)S(1)}, u32[]{:S(2)}, u32[]{:S(2)}) collective-permute-start(bf16[2,6,256,128]{3,2,1,0:T(8,128)(2,1)S(1)} %stack.4), channel_id=1, source_target_pairs={{0,4},{4,8},{8,12},{12,16},{16,20},{20,24},{24,28},{28,32},{32,36}... | collective-permute-start | bytes 2359304 | tf_op jit(solution)/shard_map/ppermute | solution.py:16
  36.8 0.6 iota_compare_fusion.3
  37.4 0.9 compare_and_fusion
  38.3 0.8 slice_bitcast_fusion
  39.1 21.5 %collective-permute-done = bf16[2,6,256,128]{3,2,1,0:T(8,128)(2,1)S(1)} collective-permute-done((bf16[2,6,256,128]{3,2,1,0:T(8,128)(2,1)S(1)}, bf16[2,6,256,128]{3,2,1,0:T(8,128)(2,1)S(1)}, u32[]{:S(2)}, u32[]{:S(2)}) %collective-permute-start) | collective-permute-done | bytes 786464 | tf_op jit(solution)/shard_map/ppermute | solution.py:16
  60.6 0.8 slice_bitcast_fusion.1
  61.4 2.3 %fusion.12 = f32[6,512,256]{2,1,0:T(8,128)} fusion(bf16[6,256,128]{2,1,0:T(8,128)(2,1)S(1)} %get-tuple-element.6, bf16[6,256,128]{2,1,0:T(8,128)(2,1)S(1)} %get-tuple-element.8, bf16[3,6,256,128]{3,2,1,0:T(8,128)(2,1)S(1)} %bitcast.52), kind=kOutput, calls=%fused_computation.23 | convolution fusion | flops 202899456 | bytes 4325376 | tf_op jit(solution)/shard_map/...qd,...kd->...qk/dot_general | solution.py:20
  63.8 0.6 copy.69
  64.4 0.3 reshape.169
  64.9 0.6 fusion.41
  65.6 1.3 fusion.9
  66.9 2.2 %convolution_convert_fusion.1 = bf16[2,2,256,128]{3,2,1,0:T(8,128)(2,1)S(1)} fusion(f32[2,2,256]{2,1,0:T(2,128)S(1)} %fusion.41, bf16[2,2,256,384]{3,2,1,0:T(8,128)(2,1)} %copy-done.1, f32[2,2,256,256]{2,3,1,0:T(8,128)} %fusion.9), kind=kOutput, calls=%fused_computation.17 | convolution fusion | flops 68027648 | bytes 2625536 | tf_op jit(solution)/shard_map/...qk,...kd->...qd/dot_general | solution.py:27
  69.3 1.0 copy.52
  70.3 13.2 %all-to-all-start.1 = ((bf16[2,512,128]{2,0,1:T(2,128)(2,1)}), bf16[2,512,128]{2,0,1:T(2,128)(2,1)}, u32[]{:S(2)}, u32[]{:S(2)}) async-start(bf16[2,512,128]{2,0,1:T(2,128)(2,1)} %copy.52), calls=%async_computation.1 | async-start | bytes 524288 | tf_op jit(solution)/shard_map/all_to_all | solution.py:79
  83.7 2.6 %fusion.40 = (f32[6,256]{1,0:T(8,128)S(1)}, f32[6,256,512]{1,2,0:T(8,128)S(1)}) fusion(f32[6,512,256]{2,1,0:T(8,128)S(1)} %copy-done, pred[256,512]{0,1:T(8,128)(4,1)} %compare_and_fusion), kind=kOutput, calls=%fused_computation.66 | output fusion | flops 4719103 | bytes 6428672 | tf_op jit(solution)/shard_map/sub | solution.py:25
  86.3 0.5 fusion.10
  86.8 12.4 %all-to-all-done.1 = bf16[2,512,128]{2,0,1:T(2,128)(2,1)} async-done(((bf16[2,512,128]{2,0,1:T(2,128)(2,1)}), bf16[2,512,128]{2,0,1:T(2,128)(2,1)}, u32[]{:S(2)}, u32[]{:S(2)}) %all-to-all-start.1) | async-done | bytes 262176 | tf_op jit(solution)/shard_map/all_to_all | solution.py:79
  99.2 1.3 convolution_convert_fusion.2
  100.5 21.4 %all-gather.2.cloned.1.call-done = bf16[1024,4096]{0,1:T(8,128)(2,1)} async-done(((bf16[1024,32]{0,1:T(8,128)(2,1)}), bf16[1024,4096]{0,1:T(8,128)(2,1)}) %all-gather.2.cloned.1.call-update) | async-done | bytes 8388624 | tf_op jit(solution)/shard_map/all_gather | solution.py:101
  121.9 7.2 %convolution_convert_fusion = bf16[256,4096]{1,0:T(8,128)(2,1)} fusion(bf16[1024,4096]{0,1:T(8,128)(2,1)} %all-gather.2.cloned.1.call-done, bf16[256,768]{0,1:T(8,128)(2,1)S(1)} %bitcast.61, bf16[256,256]{0,1:T(8,128)(2,1)S(1)} %bitcast.62), kind=kOutput, calls=%fused_computation.2 | convolution fusion | flops 2149580800 | bytes 11010048 | tf_op jit(solution)/shard_map/dot_general | solution.py:99
  129.2 31.4 %reduce-scatter.2.cloned.1.call-done = bf16[256,1024]{1,0:T(8,128)(2,1)} async-done(((bf16[256,4096]{1,0:T(8,128)(2,1)}), bf16[256,1024]{1,0:T(8,128)(2,1)}) %reduce-scatter.2.cloned.1.call-update) | async-done | bytes 524304 | tf_op jit(solution)/shard_map/reduce_scatter | solution.py:106
  (26 shorter events, 0.9 us)
Async XLA Ops:
  6.5 115.4 %all-gather.2.cloned.1.call-start = ((), (), s32[]{:S(2)}) async-start(), calls=%async_computation.3 | async-start | bytes 8454144 | tf_op jit(solution)/shard_map/all_gather | solution.py:101
  8.7 23.1 %copy-start.2 = (bf16[3,256,768]{2,1,0:T(8,128)(2,1)S(1)}, bf16[3,256,768]{2,1,0:T(8,128)(2,1)}, u32[]{:S(2)}) copy-start(bf16[3,256,768]{2,1,0:T(8,128)(2,1)} %param.6) | copy-start | bytes 3538948
  13.3 50.4 %all-to-all-start = ((bf16[2,512,384]{2,0,1:T(2,128)(2,1)}), bf16[2,512,384]{2,0,1:T(2,128)(2,1)S(1)}, u32[]{:S(2)}, u32[]{:S(2)}) async-start(bf16[2,512,384]{2,0,1:T(2,128)(2,1)} %copy.48), calls=%async_computation | async-start | bytes 1572864 | tf_op jit(solution)/shard_map/all_to_all | solution.py:61
  33.2 27.4 %collective-permute-start = (bf16[2,6,256,128]{3,2,1,0:T(8,128)(2,1)S(1)}, bf16[2,6,256,128]{3,2,1,0:T(8,128)(2,1)S(1)}, u32[]{:S(2)}, u32[]{:S(2)}) collective-permute-start(bf16[2,6,256,128]{3,2,1,0:T(8,128)(2,1)S(1)} %stack.4), channel_id=1, source_target_pairs={{0,4},{4,8},{8,12},{12,16},{16,20},{20,24},{24,28},{28,32},{32,36}... | collective-permute-start | bytes 2359304 | tf_op jit(solution)/shard_map/ppermute | solution.py:16
  61.4 3.5 %copy-start.5 = (pred[256,256]{0,1:T(8,128)(4,1)S(1)}, pred[256,256]{0,1:T(8,128)(4,1)}, u32[]{:S(2)}) copy-start(pred[256,256]{0,1:T(8,128)(4,1)} %iota_compare_fusion.3) | copy-start | bytes 196612
  64.7 0.9 copy-start.1
  66.9 16.8 %copy-start = (f32[6,512,256]{2,1,0:T(8,128)S(1)}, f32[6,512,256]{2,1,0:T(8,128)}, u32[]{:S(2)}) copy-start(f32[6,512,256]{2,1,0:T(8,128)} %fusion.12) | copy-start | bytes 9437188
  70.3 28.9 %all-to-all-start.1 = ((bf16[2,512,128]{2,0,1:T(2,128)(2,1)}), bf16[2,512,128]{2,0,1:T(2,128)(2,1)}, u32[]{:S(2)}, u32[]{:S(2)}) async-start(bf16[2,512,128]{2,0,1:T(2,128)(2,1)} %copy.52), calls=%async_computation.1 | async-start | bytes 524288 | tf_op jit(solution)/shard_map/all_to_all | solution.py:79
  83.5 2.9 %copy-start.3 = (bf16[6,256,128]{2,1,0:T(8,128)(2,1)S(1)}, bf16[6,256,128]{2,1,0:T(8,128)(2,1)}, u32[]{:S(2)}) copy-start(bf16[6,256,128]{2,1,0:T(8,128)(2,1)} %get-tuple-element.5) | copy-start | bytes 1179652
  83.5 77.0 %reduce-scatter.2.cloned.1.call-start = ((), (), s32[]{:S(2)}) async-start(), calls=%async_computation.4 | async-start | bytes 2621440 | tf_op jit(solution)/shard_map/reduce_scatter | solution.py:106
  83.7 2.6 %copy-start.4 = (bf16[6,256,128]{2,1,0:T(8,128)(2,1)S(1)}, bf16[6,256,128]{2,1,0:T(8,128)(2,1)}, u32[]{:S(2)}) copy-start(bf16[6,256,128]{2,1,0:T(8,128)(2,1)} %get-tuple-element.7) | copy-start | bytes 1179652
Sparse Core Ops, SparseCore 0:
  10.5 111.3 all-gather.1
  129.3 31.1 reduce-scatter.1
where the time goes:
time: 168 us; the launch traced here: 167 us
  waiting for transfers between devices  86.7 us (52%)
  starting transfers between devices  35.3 us (21%)
  matrix products  15.9 us (9%)
  between operations  13.6 us (8%)
  local copies, waits for them, and re-layouts  8.9 us (5%)
  other arithmetic  6.95 us (4%)
    reduce_scatter x1, waiting for transfers between devices, on_device(): lax.psum_scatter(rounded, 'head', scatter_dimension=1, tiled=True)  31.4 us
    ppermute x1, waiting for transfers between devices, shifted(): return lax.ppermute(block, axis, route)  21.5 us
    all_gather x1, waiting for transfers between devices, on_device(): lax.all_gather(proj_rows, 'seq', axis=1, tiled=True)  21.4 us
    all_to_all x1, starting transfers between devices, on_device(): lax.all_to_all(send_rows, 'seq', split_axis=1, concat_axis=1, tiled=True)  18.4 us
    all_to_all x1, starting transfers between devices, on_device(): lax.all_to_all(answered, 'seq', split_axis=1, concat_axis=1, tiled=True)  13.2 us
    all_to_all x1, waiting for transfers between devices, on_device(): lax.all_to_all(answered, 'seq', split_axis=1, concat_axis=1, tiled=True)  12.4 us
    dot_general x1, matrix products, on_device(): jnp.dot(joined, lax.all_gather(proj_rows, 'seq', axis=1, tiled=True), pre...  7.2 us
    dot_general x2, matrix products, attend(): jnp.einsum('...qd,...kd->...qk', query, keys, preferred_element_type=jnp....  3.62 us
  transfers between devices with their start and end apart: 5, of which 4 were waited for; matrix products, arithmetic and copies ran while one was open for 14% of the time, Pallas kernels for 0%

commit v1 on v0

--- a/solution.py
+++ b/solution.py
@@ -98,7 +98,9 @@
     joined = jnp.concatenate([routed_attn, local_attn], axis=1)
     terms = jnp.dot(
         joined,
-        lax.all_gather(proj_rows, "seq", axis=1, tiled=True),
+        jnp.concatenate(
+            lax.all_to_all(jnp.stack([proj_rows] * lax.axis_size("seq")), "seq", 0, 0), axis=1
+        ),
         preferred_element_type=jnp.float32,
     )
     rounded = terms.astype(jnp.bfloat16)

time: 168 us -> 405 us (2.41)
  waiting for transfers between devices: 86.7 us -> 329 us
  matrix products: 15.9 us -> 10.4 us
    ppermute x1, waiting for transfers between devices: 21.5 us -> 219 us  [shifted(): return lax.ppermute(block, axis, route)]
    reduce_scatter x1, waiting for transfers between devices: 31.4 us -> 59 us  [on_device(): lax.psum_scatter(rounded, 'head', scatter_dimension=1, tiled=True)]
    all_to_all x1, waiting for transfers between devices: 0.01 us -> 25.1 us  [on_device(): lax.all_to_all(send_rows, 'seq', split_axis=1, concat_axis=1, tiled=True)]
    all_gather x1 -> x0, waiting for transfers between devices: 21.4 us -> none  [on_device(): lax.all_gather(proj_rows, 'seq', axis=1, tiled=True)]
    all_to_all x0 -> x1, waiting for transfers between devices: none -> 12.1 us  [on_device(): lax.all_to_all(jnp.stack([proj_rows] * lax.axis_size('seq')), 'seq', 0, 0)]
    all_to_all x0 -> x1, starting transfers between devices: none -> 8.29 us  [on_device(): lax.all_to_all(jnp.stack([proj_rows] * lax.axis_size('seq')), 'seq', 0, 0)]
    all_to_all x1, starting transfers between devices: 13.2 us -> 6.81 us  [on_device(): lax.all_to_all(answered, 'seq', split_axis=1, concat_axis=1, tiled=True)]
    another operation x0 -> x1, local copies, waits for them, and re-layouts: none -> 4.28 us  [on_device(): jnp.stack([proj_rows] * lax.axis_size('seq'))]
  transfers between devices with their start and end apart: 5 -> 5, of which waited for: 4 -> 5; matrix products, arithmetic and copies ran while one was open for 14% -> 1% of each run, Pallas kernels for 0% -> 0%
where the time goes in v1:
time: 405 us
  waiting for transfers between devices  329 us (81%)
  starting transfers between devices  37.3 us (9%)
  between operations  13.6 us (3%)
  local copies, waits for them, and re-layouts  11.4 us (3%)
  matrix products  10.4 us (3%)
    ppermute x1, waiting for transfers between devices, shifted(): return lax.ppermute(block, axis, route)  219 us
    reduce_scatter x1, waiting for transfers between devices, on_device(): lax.psum_scatter(rounded, 'head', scatter_dimension=1, tiled=True)  59 us
    all_to_all x1, waiting for transfers between devices, on_device(): lax.all_to_all(send_rows, 'seq', split_axis=1, concat_axis=1, tiled=True)  25.1 us
    all_to_all x1, starting transfers between devices, on_device(): lax.all_to_all(send_rows, 'seq', split_axis=1, concat_axis=1, tiled=True)  18.4 us
    all_to_all x1, waiting for transfers between devices, on_device(): lax.all_to_all(answered, 'seq', split_axis=1, concat_axis=1, tiled=True)  14.3 us
    all_to_all x1, waiting for transfers between devices, on_device(): lax.all_to_all(jnp.stack([proj_rows] * lax.axis_size('seq')), 'seq', 0, 0)  12.1 us
    all_to_all x1, starting transfers between devices, on_device(): lax.all_to_all(jnp.stack([proj_rows] * lax.axis_size('seq')), 'seq', 0, 0)  8.29 us
  transfers between devices with their start and end apart: 5, of which 5 were waited for; matrix products, arithmetic and copies ran while one was open for 1% of the time, Pallas kernels for 0%

profile of v1, /device:TPU:1, one launch (start us, length us, event | category | flops | bytes accessed | tf_op | source)
XLA Modules:
  0.0 405.0 jit_solution(14511276370171477421)
XLA Ops:
  6.6 0.7 copy.71
  7.3 0.2 convert_reduce_fusion.1
  7.5 0.7 multiply_add_fusion
  8.2 1.2 copy.46
  9.4 0.2 convert_reduce_fusion
  9.6 0.4 add_convert_fusion
  10.1 1.7 copy.49
  11.8 18.4 %all-to-all-start = ((bf16[2,512,384]{2,0,1:T(2,128)(2,1)}), bf16[2,512,384]{2,0,1:T(2,128)(2,1)S(1)}, u32[]{:S(2)}, u32[]{:S(2)}) async-start(bf16[2,512,384]{2,0,1:T(2,128)(2,1)} %copy.49), calls=%async_computation | async-start | bytes 1572864 | tf_op jit(solution)/shard_map/all_to_all | solution.py:61
  30.2 25.1 %all-to-all-done = bf16[2,512,384]{2,0,1:T(2,128)(2,1)S(1)} async-done(((bf16[2,512,384]{2,0,1:T(2,128)(2,1)}), bf16[2,512,384]{2,0,1:T(2,128)(2,1)S(1)}, u32[]{:S(2)}, u32[]{:S(2)}) %all-to-all-start) | async-done | bytes 786464 | tf_op jit(solution)/shard_map/all_to_all | solution.py:61
  55.3 0.6 copy.70
  55.9 0.3 reshape.177
  56.2 0.2 compare_reduce_fusion
  56.5 0.6 fusion.41
  57.0 0.3 fusion.9
  57.4 0.5 convolution_convert_fusion.1
  58.1 1.0 copy.53
  59.0 6.8 %all-to-all-start.1 = ((bf16[2,512,128]{2,0,1:T(2,128)(2,1)}), bf16[2,512,128]{2,0,1:T(2,128)(2,1)S(1)}, u32[]{:S(2)}, u32[]{:S(2)}) async-start(bf16[2,512,128]{2,0,1:T(2,128)(2,1)} %copy.53), calls=%async_computation.1 | async-start | bytes 524288 | tf_op jit(solution)/shard_map/all_to_all | solution.py:79
  65.9 14.3 %all-to-all-done.1 = bf16[2,512,128]{2,0,1:T(2,128)(2,1)S(1)} async-done(((bf16[2,512,128]{2,0,1:T(2,128)(2,1)}), bf16[2,512,128]{2,0,1:T(2,128)(2,1)S(1)}, u32[]{:S(2)}, u32[]{:S(2)}) %all-to-all-start.1) | async-done | bytes 262176 | tf_op jit(solution)/shard_map/all_to_all | solution.py:79
  80.2 4.3 %stack.5 = bf16[128,1024,32]{1,2,0:T(8,128)(2,1)} broadcast(bf16[1024,32]{0,1:T(8,128)(2,1)S(1)} %pad_maximum_fusion), dimensions={1,2} | broadcast | bytes 8454144 | tf_op jit(solution)/shard_map/stack | solution.py:102
  84.5 8.3 %all-to-all-start.2 = ((bf16[128,1024,32]{1,2,0:T(8,128)(2,1)}), bf16[128,1024,32]{1,2,0:T(8,128)(2,1)}, u32[]{:S(2)}, u32[]{:S(2)}) async-start(bf16[128,1024,32]{1,2,0:T(8,128)(2,1)} %stack.5), calls=%async_computation.2 | async-start | bytes 16777216 | tf_op jit(solution)/shard_map/all_to_all | solution.py:102
  92.8 0.2 reduce-scatter.2.cloned.1.call-start
  93.0 0.6 copy.55
  93.7 0.7 copy.56
  94.5 3.5 collective-permute-start
  98.4 218.5 %collective-permute-done = bf16[2,6,256,128]{3,2,1,0:T(8,128)(2,1)S(1)} collective-permute-done((bf16[2,6,256,128]{3,2,1,0:T(8,128)(2,1)S(1)}, bf16[2,6,256,128]{3,2,1,0:T(8,128)(2,1)S(1)}, u32[]{:S(2)}, u32[]{:S(2)}) %collective-permute-start) | collective-permute-done | bytes 786464 | tf_op jit(solution)/shard_map/ppermute | solution.py:16
  317.0 0.6 fusion.12
  317.5 1.4 fusion.40
  319.0 0.5 fusion.10
  319.5 0.3 convolution_convert_fusion.2
  319.8 12.1 %all-to-all-done.2 = bf16[128,1024,32]{1,2,0:T(8,128)(2,1)} async-done(((bf16[128,1024,32]{1,2,0:T(8,128)(2,1)}), bf16[128,1024,32]{1,2,0:T(8,128)(2,1)}, u32[]{:S(2)}, u32[]{:S(2)}) %all-to-all-start.2) | async-done | bytes 8388640 | tf_op jit(solution)/shard_map/all_to_all | solution.py:102
  332.0 7.2 %convolution_convert_fusion = bf16[256,4096]{1,0:T(8,128)(2,1)} fusion(bf16[1024,4096]{0,1:T(8,128)(2,1)} %bitcast.21, bf16[256,768]{0,1:T(8,128)(2,1)S(1)} %bitcast.64, bf16[256,256]{0,1:T(8,128)(2,1)S(1)} %bitcast.65), kind=kOutput, calls=%fused_computation.2 | convolution fusion | flops 2149580800 | bytes 11010048 | tf_op jit(solution)/shard_map/dot_general | solution.py:99
  339.2 59.0 %reduce-scatter.2.cloned.1.call-done = bf16[256,1024]{1,0:T(8,128)(2,1)} async-done(((bf16[256,4096]{1,0:T(8,128)(2,1)}), bf16[256,1024]{1,0:T(8,128)(2,1)}) %reduce-scatter.2.cloned.1.call-update) | async-done | bytes 524304 | tf_op jit(solution)/shard_map/reduce_scatter | solution.py:108
  (20 shorter events, 0.7 us)
Async XLA Ops:
  11.8 43.6 %all-to-all-start = ((bf16[2,512,384]{2,0,1:T(2,128)(2,1)}), bf16[2,512,384]{2,0,1:T(2,128)(2,1)S(1)}, u32[]{:S(2)}, u32[]{:S(2)}) async-start(bf16[2,512,384]{2,0,1:T(2,128)(2,1)} %copy.49), calls=%async_computation | async-start | bytes 1572864 | tf_op jit(solution)/shard_map/all_to_all | solution.py:61
  57.4 8.5 %copy-start.1 = (bf16[768,32]{0,1:T(8,128)(2,1)S(1)}, bf16[768,32]{0,1:T(8,128)(2,1)}, u32[]{:S(2)}) copy-start(bf16[768,32]{0,1:T(8,128)(2,1)} %param.9) | copy-start | bytes 147460
  57.4 8.5 %copy-start.2 = (bf16[256,32]{0,1:T(8,128)(2,1)S(1)}, bf16[256,32]{0,1:T(8,128)(2,1)}, u32[]{:S(2)}) copy-start(bf16[256,32]{0,1:T(8,128)(2,1)} %param.8) | copy-start | bytes 49156
  59.0 21.2 %all-to-all-start.1 = ((bf16[2,512,128]{2,0,1:T(2,128)(2,1)}), bf16[2,512,128]{2,0,1:T(2,128)(2,1)S(1)}, u32[]{:S(2)}, u32[]{:S(2)}) async-start(bf16[2,512,128]{2,0,1:T(2,128)(2,1)} %copy.53), calls=%async_computation.1 | async-start | bytes 524288 | tf_op jit(solution)/shard_map/all_to_all | solution.py:79
  84.5 8.5 %copy-start = (bf16[3,256,768]{2,1,0:T(8,128)(2,1)S(1)}, bf16[3,256,768]{2,1,0:T(8,128)(2,1)}, u32[]{:S(2)}) copy-start(bf16[3,256,768]{2,1,0:T(8,128)(2,1)} %param.6) | copy-start | bytes 3538948
  84.5 247.5 %all-to-all-start.2 = ((bf16[128,1024,32]{1,2,0:T(8,128)(2,1)}), bf16[128,1024,32]{1,2,0:T(8,128)(2,1)}, u32[]{:S(2)}, u32[]{:S(2)}) async-start(bf16[128,1024,32]{1,2,0:T(8,128)(2,1)} %stack.5), calls=%async_computation.2 | async-start | bytes 16777216 | tf_op jit(solution)/shard_map/all_to_all | solution.py:102
  92.8 305.4 %reduce-scatter.2.cloned.1.call-start = ((), (), s32[]{:S(2)}) async-start(), calls=%async_computation.4 | async-start | bytes 2621440 | tf_op jit(solution)/shard_map/reduce_scatter | solution.py:108
  94.5 222.4 %collective-permute-start = (bf16[2,6,256,128]{3,2,1,0:T(8,128)(2,1)S(1)}, bf16[2,6,256,128]{3,2,1,0:T(8,128)(2,1)S(1)}, u32[]{:S(2)}, u32[]{:S(2)}) collective-permute-start(bf16[2,6,256,128]{3,2,1,0:T(8,128)(2,1)S(1)} %stack.6), channel_id=1, source_target_pairs={{0,4},{4,8},{8,12},{12,16},{16,20},{20,24},{24,28},{28,32},{32,36}... | collective-permute-start | bytes 2359304 | tf_op jit(solution)/shard_map/ppermute | solution.py:16
Sparse Core Ops, SparseCore 0:
  339.3 58.8 reduce-scatter.1
